TPU v7x, 32 devices: a whole 2x2x4 slice. The times are simulated.
32 devices in a mesh: seq: 8 (over z, core), chan: 4 (over y, x).
Axes of the slice: x: 2, y: 2, z: 4, core: 2. Of those that a mesh axis runs over, the one named last changes fastest.
Arguments:
- tokens: bfloat16 [2560, 4096], P('seq', 'chan'), may hold values from -70 to 70
- in_weight: bfloat16 [4096, 3, 4096], P(None, None, 'chan'), may hold values from -0.09375 to 0.09375
- short_filter: float32 [3, 3, 4096], P(None, None, 'chan'), may hold values from -2 to 2
- long_filter: bfloat16 [256, 128], P('chan'), may hold values from -0.5 to 0.5
- skip_gain: float32 [4096], P('chan'), may hold values from -4 to 4
- out_weight: bfloat16 [4096, 4096], P('chan'), may hold values from -0.125 to 0.125
Outputs:
- mixed: bfloat16 [2560, 4096], P('seq', 'chan')
All inputs are finite; a program needn't handle non-finite values.
Results may differ from a plain program's by a relative error of at most 0.018.
Values may be sent and summed in bfloat16 or wider, within the bound.
A program may use at most 128 MiB of HBM per device.

v0:
```python
import math

import jax
import jax.numpy as jnp
from jax import lax
from jax.sharding import PartitionSpec as P


def shifted(value, axis, steps):
    count = lax.axis_size(axis)
    leading, last = (max(0, -steps), min(count, count - steps))
    return lax.ppermute(value, axis, [(source, source + steps) for source in range(leading, last)])


def featurize(extended, short_taps, out_count):
    tap_count = short_taps.shape[0]
    summed = jnp.zeros((out_count, short_taps.shape[1]), jnp.float32)
    for step_back in range(tap_count):
        lower = tap_count - 1 - step_back
        summed = summed + short_taps[step_back] * extended[lower : lower + out_count].astype(
            jnp.float32
        )
    return summed


def body(tokens, in_weight, short_filter, long_filter, skip_gain, out_weight):
    row_count = tokens.shape[0]
    model_width = in_weight.shape[0]
    chan_count = in_weight.shape[2]
    flat_weight = in_weight.reshape(model_width, 3 * chan_count)
    panel = lax.all_gather(tokens, "chan", axis=1, tiled=True)
    summed = jnp.dot(panel, flat_weight, preferred_element_type=jnp.float32)
    widened = panel.astype(jnp.float32)
    summed, squares = (summed, jnp.sum(widened * widened, axis=1, keepdims=True))
    projected = (summed * lax.rsqrt(squares / model_width + 1e-06)).astype(jnp.bfloat16)
    short_taps = short_filter.reshape(short_filter.shape[0], 3 * chan_count)
    tap_count = short_filter.shape[0]
    filter_reach = long_filter.shape[1] - 1
    edge_rows = shifted(projected[row_count - filter_reach - tap_count + 1 :], "seq", 1)
    extended = jnp.concatenate([edge_rows, projected], axis=0)
    features = featurize(extended, short_taps, row_count + filter_reach)
    queries = features[filter_reach:, :chan_count]
    padded = (features[:, chan_count : 2 * chan_count] * features[:, 2 * chan_count :]).astype(
        jnp.bfloat16
    )
    gated_rows = padded[filter_reach:]
    groups = long_filter.shape[0]
    group_size = chan_count // groups
    block_rows = math.gcd(row_count, 256)
    lag_table = (
        jnp.arange(block_rows, dtype=jnp.int32)[:, None]
        + filter_reach
        - jnp.arange(block_rows + filter_reach, dtype=jnp.int32)[None, :]
    )
    inside = (lag_table >= 0) & (lag_table <= filter_reach)
    toeplitz = jnp.where(
        inside[None],
        jnp.take(long_filter, jnp.clip(lag_table, 0, filter_reach), axis=1),
        jnp.zeros((), jnp.bfloat16),
    )
    grouped = padded.reshape(row_count + filter_reach, groups, group_size)

    def one_block(block_index):
        window_rows = lax.dynamic_slice_in_dim(
            grouped, block_index * block_rows, block_rows + filter_reach, 0
        )
        return jnp.einsum("gts,sgc->tgc", toeplitz, window_rows, preferred_element_type=jnp.float32)

    long_mixed = lax.map(one_block, jnp.arange(row_count // block_rows, dtype=jnp.int32)).reshape(
        row_count, chan_count
    )
    long_mixed = long_mixed + skip_gain * gated_rows.astype(jnp.float32)
    hidden = (queries * long_mixed).astype(jnp.bfloat16)
    partial_terms = jnp.dot(hidden, out_weight, preferred_element_type=jnp.float32)
    mixed_out = lax.psum_scatter(
        partial_terms.astype(jnp.bfloat16), "chan", scatter_dimension=1, tiled=True
    )
    return mixed_out


def solution(mesh):
    in_specs = (
        P("seq", "chan"),
        P(None, None, "chan"),
        P(None, None, "chan"),
        P("chan", None),
        P("chan"),
        P("chan", None),
    )
    out_specs = P("seq", "chan")
    return jax.shard_map(body, mesh=mesh, in_specs=in_specs, out_specs=out_specs, check_vma=False)
```

profile of v0, /device:TPU:0, one launch (start us, length us, event | category | flops | bytes accessed | tf_op | source)
XLA Modules:
  0.0 278.4 jit_solution(17276946775811575660)
XLA Ops:
  6.5 0.0 all-gather.2.cloned.1.call-start
  6.5 0.7 all-gather.2.cloned.1.call-update
  7.3 0.0 reduce-scatter.2.cloned.1.call-start
  7.3 31.9 %copy.11 = bf16[4096,3,1024]{0,2,1:T(8,128)(2,1)} copy(bf16[4096,3,1024]{2,0,1:T(8,128)(2,1)} %param.9) | data formatting | bytes 50331648 | tf_op args[1]
  39.2 0.1 compare_select_fusion
  39.3 12.3 %all-gather.2.cloned.1.call-done = bf16[320,4096]{1,0:T(8,128)(2,1)} async-done(((bf16[320,1024]{1,0:T(8,128)(2,1)}), bf16[320,4096]{1,0:T(8,128)(2,1)}) %all-gather.2.cloned.1.call-update) | async-done | bytes 2621456 | tf_op jit(solution)/shard_map/all_gather | solution.py:31
  51.6 2.3 multiply_reduce_fusion
  53.9 0.0 copy-start.3
  53.9 0.0 copy-start.4
  54.0 13.9 %fusion.3 = bf16[320,3072]{1,0:T(8,128)(2,1)S(1)} fusion(bf16[320,4096]{1,0:T(8,128)(2,1)} %all-gather.2.cloned.1.call-done, bf16[4096,3072]{0,1:T(8,128)(2,1)} %bitcast.27, f32[320]{0:T(512)S(1)} %add_rsqrt_fusion), kind=kOutput, calls=%fused_computation.8 | convolution fusion | flops 8055029760 | bytes 29754624 | tf_op jit(solution)/shard_map/dot_general | solution.py:32
  67.9 0.0 copy-start.1
  67.9 1.3 slice.49
  69.2 2.6 collective-permute-start
  71.8 0.0 copy-done.3
  71.9 0.0 copy-done.1
  71.9 0.2 reshape.119
  72.1 0.0 copy-done.4
  72.1 0.1 copy.13
  72.3 36.5 %gather_fusion = bf16[12224,64]{1,0:T(8,128)(2,1)S(1)} fusion(bf16[64,128]{0,1:T(8,128)(2,1)S(1)} %copy.13, s32[12288]{0:T(1024)S(1)} %pad_clamp_fusion), kind=kCustom, calls=%fused_computation | custom fusion | bytes 3178240 | tf_op jit(solution)/shard_map/jit(_take)/gather | solution.py:58
  108.8 2.8 %copy.14 = bf16[12224,64]{0,1:T(8,128)(2,1)} copy(bf16[12224,64]{1,0:T(8,128)(2,1)S(1)} %gather_fusion) | data formatting | bytes 3129344 | tf_op jit(solution)/shard_map/jit(_take)/gather | solution.py:58
  111.6 8.0 %reshape.122 = bf16[64,191,64]{1,0,2:T(8,128)(2,1)} reshape(bf16[12224,64]{0,1:T(8,128)(2,1)} %copy.14) | data formatting | bytes 3129344 | tf_op jit(solution)/shard_map/jit(_take)/gather | solution.py:58
  119.6 0.0 copy-start.2
  119.6 0.1 fusion.15
  119.7 1.9 select_bitcast_fusion
  121.7 0.0 collective-permute-done
  121.7 0.1 copy-done.2
  121.8 4.0 %multiply_add_fusion = f32[447,3072]{1,0:T(8,128)S(1)} fusion(bf16[320,3072]{1,0:T(8,128)(2,1)S(1)} %copy-done.2, bf16[129,3072]{1,0:T(8,128)(2,1)} %collective-permute-done, f32[3072]{0:T(1024)S(1)} %mul.70, f32[3072]{0:T(1024)S(1)} %mul.67, f32[3072]{0:T(1024)S(1)} %mul.61), kind=kLoop, calls=%fused_computation.4 | loop fusion | flops 23344128 | bytes 8288256 | tf_op jit(solution)/shard_map/add | solution.py:20
  125.8 0.0 copy-start
  125.8 2.4 copy-done
  128.2 0.3 fusion.6
  128.5 1.3 copy.12
  129.8 88.7 %while.10 = (s32[]{:T(128)}, f32[5,64,64,16]{1,0,3,2:T(8,128)}, s32[5]{0:T(128)S(1)}, bf16[447,64,16]{0,2,1:T(8,128)(2,1)}, bf16[64,64,191]{2,1,0:T(8,128)(2,1)S...) while((s32[]{:T(128)}, f32[5,64,64,16]{1,0,3,2:T(8,128)}, s32[5]{0:T(128)S(1)}, ...), condition=%wide.region_2.3_spmd, body=%wide.region_1.2_spmd.sunk | while | flops 25034756 | bytes 2875551 | solution.py:69
  129.8 0.7 dynamic_slice.12
  131.2 1.8 fusion.27
  133.0 14.6 %dynamic_update_slice.5 = f32[5,64,64,16]{1,0,3,2:T(8,128)} dynamic-update-slice(f32[5,64,64,16]{1,0,3,2:T(8,128)} %get-tuple-element.94, f32[1,64,64,16]{1,0,3,2:T(1,128)S(1)} %bitcast.26, s32[]{:T(128)} %get-tuple-element.93, s32[]{:T(128)} %constant.23.clone.1..sunk, s32[]{:T(128)} %constant.23.clone.1..sunk, s32[]{:T(128)} %constant.23.clone.1..sunk) | dynamic-update-slice | bytes 524292 | tf_op jit(solution)/shard_map/while/body/jit(dynamic_update_index_in_dim)/dynamic_update_slice | solution.py:69
  147.6 0.7 dynamic_slice.12
  148.9 1.8 fusion.27
  150.8 14.6 %dynamic_update_slice.5 = f32[5,64,64,16]{1,0,3,2:T(8,128)} dynamic-update-slice(f32[5,64,64,16]{1,0,3,2:T(8,128)} %get-tuple-element.94, f32[1,64,64,16]{1,0,3,2:T(1,128)S(1)} %bitcast.26, s32[]{:T(128)} %get-tuple-element.93, s32[]{:T(128)} %constant.23.clone.1..sunk, s32[]{:T(128)} %constant.23.clone.1..sunk, s32[]{:T(128)} %constant.23.clone.1..sunk) | dynamic-update-slice | bytes 524292 | tf_op jit(solution)/shard_map/while/body/jit(dynamic_update_index_in_dim)/dynamic_update_slice | solution.py:69
  165.4 0.7 dynamic_slice.12
  166.7 1.8 fusion.27
  168.5 14.6 %dynamic_update_slice.5 = f32[5,64,64,16]{1,0,3,2:T(8,128)} dynamic-update-slice(f32[5,64,64,16]{1,0,3,2:T(8,128)} %get-tuple-element.94, f32[1,64,64,16]{1,0,3,2:T(1,128)S(1)} %bitcast.26, s32[]{:T(128)} %get-tuple-element.93, s32[]{:T(128)} %constant.23.clone.1..sunk, s32[]{:T(128)} %constant.23.clone.1..sunk, s32[]{:T(128)} %constant.23.clone.1..sunk) | dynamic-update-slice | bytes 524292 | tf_op jit(solution)/shard_map/while/body/jit(dynamic_update_index_in_dim)/dynamic_update_slice | solution.py:69
  183.1 0.7 dynamic_slice.12
  184.4 1.8 fusion.27
  186.3 14.6 %dynamic_update_slice.5 = f32[5,64,64,16]{1,0,3,2:T(8,128)} dynamic-update-slice(f32[5,64,64,16]{1,0,3,2:T(8,128)} %get-tuple-element.94, f32[1,64,64,16]{1,0,3,2:T(1,128)S(1)} %bitcast.26, s32[]{:T(128)} %get-tuple-element.93, s32[]{:T(128)} %constant.23.clone.1..sunk, s32[]{:T(128)} %constant.23.clone.1..sunk, s32[]{:T(128)} %constant.23.clone.1..sunk) | dynamic-update-slice | bytes 524292 | tf_op jit(solution)/shard_map/while/body/jit(dynamic_update_index_in_dim)/dynamic_update_slice | solution.py:69
  200.9 0.7 dynamic_slice.12
  202.2 1.7 fusion.27
  203.9 14.6 %dynamic_update_slice.5 = f32[5,64,64,16]{1,0,3,2:T(8,128)} dynamic-update-slice(f32[5,64,64,16]{1,0,3,2:T(8,128)} %get-tuple-element.94, f32[1,64,64,16]{1,0,3,2:T(1,128)S(1)} %bitcast.26, s32[]{:T(128)} %get-tuple-element.93, s32[]{:T(128)} %constant.23.clone.1..sunk, s32[]{:T(128)} %constant.23.clone.1..sunk, s32[]{:T(128)} %constant.23.clone.1..sunk) | dynamic-update-slice | bytes 524292 | tf_op jit(solution)/shard_map/while/body/jit(dynamic_update_index_in_dim)/dynamic_update_slice | solution.py:69
  218.5 0.0 copy-start.5
  218.5 3.2 %reshape.116 = f32[320,1024]{0,1:T(8,128)S(1)} reshape(f32[5,64,64,16]{1,0,3,2:T(8,128)} %get-tuple-element.32) | data formatting | bytes 2621440 | tf_op jit(solution)/shard_map/reshape | solution.py:69
  221.7 1.6 copy.16
  223.3 0.0 copy-done.5
  223.3 8.6 %convolution_convert_fusion = bf16[320,4096]{1,0:T(8,128)(2,1)} fusion(bf16[1024,4096]{1,0:T(8,128)(2,1)} %param.13, f32[447,3072]{1,0:T(8,128)} %copy-done, f32[320,1024]{1,0:T(8,128)} %copy.16, bf16[447,1024]{1,0:T(8,128)(2,1)S(1)} %fusion.6, f32[1024]{0:T(1024)S(1)} %copy-done.5), kind=kOutput, calls=%fused_computation.5 | convolution fusion | flops 2687303680 | bytes 14290944 | tf_op jit(solution)/shard_map/dot_general | solution.py:74
  232.0 0.0 reduce-scatter.2.cloned.1.call-update
  232.0 39.5 %reduce-scatter.2.cloned.1.call-done = bf16[320,1024]{1,0:T(8,128)(2,1)} async-done(((bf16[320,4096]{1,0:T(8,128)(2,1)}), bf16[320,1024]{1,0:T(8,128)(2,1)}) %reduce-scatter.2.cloned.1.call-update) | async-done | bytes 655376 | tf_op jit(solution)/shard_map/reduce_scatter | solution.py:75
  (9 shorter events, 0.1 us)
Async XLA Ops:
  6.5 45.0 %all-gather.2.cloned.1.call-start = ((), (), s32[]{:S(2)}) async-start(), calls=%async_computation.1 | async-start | bytes 3276800 | tf_op jit(solution)/shard_map/all_gather | solution.py:31
  7.3 264.3 %reduce-scatter.2.cloned.1.call-start = ((), (), s32[]{:S(2)}) async-start(), calls=%async_computation.2 | async-start | bytes 3276800 | tf_op jit(solution)/shard_map/reduce_scatter | solution.py:75
  53.9 17.9 %copy-start.3 = (f32[3,3,1024]{2,1,0:T(4,128)S(1)}, f32[3,3,1024]{2,1,0:T(4,128)}, u32[]{:S(2)}) copy-start(f32[3,3,1024]{2,1,0:T(4,128)} %param.10) | copy-start | bytes 110596
  53.9 18.2 %copy-start.4 = (bf16[64,128]{1,0:T(8,128)(2,1)S(1)}, bf16[64,128]{1,0:T(8,128)(2,1)}, u32[]{:S(2)}) copy-start(bf16[64,128]{1,0:T(8,128)(2,1)} %param.11) | copy-start | bytes 49156
  67.9 4.0 %copy-start.1 = (bf16[320,3072]{1,0:T(8,128)(2,1)}, bf16[320,3072]{1,0:T(8,128)(2,1)S(1)}, u32[]{:S(2)}) copy-start(bf16[320,3072]{1,0:T(8,128)(2,1)S(1)} %fusion.3) | copy-start | bytes 5898244
  69.2 52.5 %collective-permute-start = (bf16[129,3072]{1,0:T(8,128)(2,1)}, bf16[129,3072]{1,0:T(8,128)(2,1)}, u32[]{:S(2)}, u32[]{:S(2)}) collective-permute-start(bf16[129,3072]{1,0:T(8,128)(2,1)} %slice.49), channel_id=1, source_target_pairs={{0,4},{4,8},{8,12},{12,16},{16,20},{20,24},{24,28},{1,5},{5,9},{9,... | collective-permute-start | bytes 2377736 | tf_op jit(solution)/shard_map/ppermute | solution.py:12
  119.6 2.2 copy-start.2
  125.8 2.4 copy-start
  218.5 4.8 %copy-start.5 = (f32[1024]{0:T(1024)S(1)}, f32[1024]{0:T(1024)}, u32[]{:S(2)}) copy-start(f32[1024]{0:T(1024)} %param.12) | copy-start | bytes 12292
Sparse Core Ops, SparseCore 0:
  9.2 42.3 all-gather.1
  232.1 39.3 reduce-scatter.1
where the time goes:
time: 281 us; the launch traced here: 278 us
  local copies, waits for them, and re-layouts  166 us (59%)
  waiting for transfers between devices  52.5 us (19%)
  matrix products  31.6 us (11%)
  between operations  13.6 us (5%)
  other arithmetic  8.77 us (3%)
  loops' own time  3.43 us (1%)
    dynamic_update_slice x5, local copies, waits for them, and re-layouts, body(): lax.map(one_block, jnp.arange(row_count // block_rows, dtype=jnp.int32))  72.9 us
    gather x3, local copies, waits for them, and re-layouts, body(): jnp.take(long_filter, jnp.clip(lag_table, 0, filter_reach), axis=1)  47.3 us
    reduce_scatter x1, waiting for transfers between devices, body(): lax.psum_scatter(partial_terms.astype(jnp.bfloat16), 'chan', scatter_dime...  39.5 us
    unnamed x14, local copies, waits for them, and re-layouts  34.6 us
    dot_general x1, matrix products, body(): summed = jnp.dot(panel, flat_weight, preferred_element_type=jnp.float32)  13.9 us
    all_gather x1, waiting for transfers between devices, body(): panel = lax.all_gather(tokens, 'chan', axis=1, tiled=True)  12.3 us
    dot_general x5, matrix products, one_block(): jnp.einsum('gts,sgc->tgc', toeplitz, window_rows, preferred_element_type=...  9.07 us
    dot_general x1, matrix products, body(): jnp.dot(hidden, out_weight, preferred_element_type=jnp.float32)  8.64 us
  transfers between devices with their start and end apart: 3, of which 2 were waited for; matrix products, arithmetic and copies ran while one was open for 29% of the time, Pallas kernels for 0%

commit v1 on v0

v1 whole, which is shorter than its diff:
```python
import functools

import jax
import jax.numpy as jnp
from jax import lax
from jax.experimental import pallas as pl
from jax.experimental.pallas import tpu as pltpu
from jax.sharding import PartitionSpec as P

MESH = pl.DeviceIdType.MESH
F32, BF16 = jnp.float32, jnp.bfloat16
PAD = 8


def kernel(
    n_seq, n_chan, tok, w_hbm, sf, lf, skip, wo_hbm, out,
    panel, wv, wo, acc, ssq, rev, toep, gext, tail, halo_p, hid, psend, precv,
    w_sem, wo_sem, ag_send, ag_recv, rs_send, rs_recv, halo_send, halo_recv,
):
    rows, kc = tok.shape
    cc = w_hbm.shape[2]
    oc = out.shape[1]
    groups, taps = lf.shape
    gsize = cc // groups
    ct = min(256, cc)
    tiles = cc // ct
    gpt = ct // gsize
    ot = min(256, oc)
    model = kc * n_chan
    seq = lax.axis_index("seq")
    chan = lax.axis_index("chan")
    width = 2 if n_chan % 2 == 0 else 1
    height = n_chan // width
    my_y, my_x = chan // width, lax.rem(chan, width)

    def at_offset(d, sign):
        dy, dx = d // width, d % width
        y = lax.rem(my_y + sign * dy + height, height)
        x = lax.rem(my_x + sign * dx + width, width)
        return y * width + x

    target = [at_offset(d, 1) for d in range(n_chan)]
    source = [at_offset(d, -1) for d in range(n_chan)]

    def w_copy(d):
        return pltpu.make_async_copy(
            w_hbm.at[:, pl.ds(pl.multiple_of(source[d] * kc, kc), kc), :], wv.at[d], w_sem.at[d]
        )

    def wo_copy(d):
        return pltpu.make_async_copy(
            wo_hbm.at[:, pl.ds(pl.multiple_of(target[d] * oc, oc), oc)], wo.at[d], wo_sem.at[d]
        )

    def ag_copy(d):
        return pltpu.make_async_remote_copy(
            src_ref=tok, dst_ref=panel.at[d - 1],
            send_sem=ag_send.at[d - 1], recv_sem=ag_recv.at[d - 1],
            device_id=(seq, target[d]), device_id_type=MESH,
        )

    def halo_copy(which):
        src, dst = (
            (tail, halo_p) if which == 0 else (gext.at[pl.ds(rows, taps)], gext.at[pl.ds(0, taps)])
        )
        return pltpu.make_async_remote_copy(
            src_ref=src, dst_ref=dst,
            send_sem=halo_send.at[which], recv_sem=halo_recv.at[which],
            device_id=(lax.rem(seq + 1, n_seq), chan), device_id_type=MESH,
        )

    def rs_copy(part, r0, r1, d):
        return pltpu.make_async_remote_copy(
            src_ref=psend.at[d - 1, pl.ds(r0, r1 - r0)], dst_ref=precv.at[d - 1, pl.ds(r0, r1 - r0)],
            send_sem=rs_send.at[part, d - 1], recv_sem=rs_recv.at[part, d - 1],
            device_id=(seq, target[d]), device_id_type=MESH,
        )

    w_copy(0).start()
    barrier = pltpu.get_barrier_semaphore()
    for d in range(1, n_chan):
        pl.semaphore_signal(barrier, inc=1, device_id=(seq, target[d]), device_id_type=MESH)

    @pl.when(seq > 0)
    def _():
        pl.semaphore_signal(barrier, inc=1, device_id=(seq - 1, chan), device_id_type=MESH)

    @pl.when(seq < n_seq - 1)
    def _():
        pl.semaphore_signal(barrier, inc=1, device_id=(seq + 1, chan), device_id_type=MESH)

    arrivals = n_chan - 1 + (seq > 0).astype(jnp.int32) + (seq < n_seq - 1).astype(jnp.int32)
    pl.semaphore_wait(barrier, arrivals)

    for d in range(n_chan - 1, 0, -1):
        ag_copy(d).start()
    for d in range(1, n_chan):
        w_copy(d).start()
    for d in range(n_chan):
        wo_copy(d).start()

    def add_squares(ref, first):
        total = jnp.zeros((rows, 128), F32)
        for c in range(0, kc, 128):
            part = ref[:, c : c + 128].astype(F32)
            total = total + part * part
        ssq[...] = total if first else ssq[...] + total

    def col(j, size):
        return pl.ds(pl.multiple_of(j * size, size), size)

    add_squares(tok, True)
    w_copy(0).wait()

    @pl.loop(0, tiles)
    def _(j):
        for i in range(3):
            acc[i, PAD : PAD + rows, col(j, ct)] = jnp.dot(
                tok[...], wv[0, i, :, col(j, ct)], preferred_element_type=F32
            )

    lag = lax.broadcasted_iota(jnp.int32, (taps, 2 * taps), 0)
    place = lax.broadcasted_iota(jnp.int32, (taps, 2 * taps), 1)
    flip = jnp.where(lag + place == taps, 1.0, 0.0).astype(BF16)
    rev[...] = jnp.dot(lf[...], flip, preferred_element_type=F32)

    @pl.loop(0, groups)
    def _(g):
        line = jnp.broadcast_to(rev[pl.ds(g, 1), :], (taps, 2 * taps))
        toep[g] = pltpu.roll(line, 0, 1, stride=1, stride_axis=0).astype(BF16)

    gext[pl.ds(taps + rows, gext.shape[0] - taps - rows), :] = jnp.zeros(
        (gext.shape[0] - taps - rows, cc), BF16
    )

    for d in range(1, n_chan):
        ag_copy(d).wait_recv()
        w_copy(d).wait()
        add_squares(panel.at[d - 1], False)
        if d < n_chan - 1:

            @pl.loop(0, tiles)
            def _(j):
                for i in range(3):
                    acc[i, PAD : PAD + rows, col(j, ct)] += jnp.dot(
                        panel[d - 1], wv[d, i, :, col(j, ct)], preferred_element_type=F32
                    )

    last = n_chan - 1
    inverse = lax.rsqrt(jnp.sum(ssq[...], axis=1, keepdims=True) * (1.0 / model) + 1e-6)
    ssq[...] = jnp.broadcast_to(inverse, (rows, 128))

    @pl.loop(0, tiles)
    def _(j):
        scale = ssq[:, 0:1]
        for i in range(3):
            summed = acc[i, PAD : PAD + rows, col(j, ct)] + jnp.dot(
                panel[last - 1], wv[last, i, :, col(j, ct)], preferred_element_type=F32
            )
            projected = (summed * scale).astype(BF16)
            acc[i, PAD : PAD + rows, col(j, ct)] = projected.astype(F32)
            tail[i, :, col(j, ct)] = projected[rows - 16 :]

    @pl.when(seq < n_seq - 1)
    def _():
        halo_copy(0).start()

    def feature(i, r0, r1, c):
        total = sf[0, i : i + 1, c] * acc[i, PAD + r0 : PAD + r1, c]
        for step in range(1, sf.shape[0]):
            total = total + sf[step, i : i + 1, c] * acc[i, PAD + r0 - step : PAD + r1 - step, c]
        return total

    def gate(r0, r1):
        @pl.loop(0, tiles)
        def _(j):
            c = col(j, ct)
            gext[taps + r0 : taps + r1, c] = (feature(1, r0, r1, c) * feature(2, r0, r1, c)).astype(BF16)

    gate(rows - taps, rows)

    @pl.when(seq < n_seq - 1)
    def _():
        halo_copy(1).start()

    gate(16, rows - taps)

    @pl.when(seq > 0)
    def _():
        halo_copy(0).wait_recv()
        for i in range(3):
            acc[i, 0:PAD, :] = halo_p[i, 16 - PAD : 16, :].astype(F32)

    @pl.when(seq == 0)
    def _():
        acc[:, 0:PAD, :] = jnp.zeros((3, PAD, cc), F32)
        gext[0:taps, :] = jnp.zeros((taps, cc), BF16)

    gate(0, 16)

    def long_filter(r0, size):
        @pl.loop(0, tiles)
        def _(j):
            c = col(j, ct)
            table = toep[pl.ds(j * gpt, gpt), 0:size, :].reshape(gpt * size, 2 * taps)
            full = jnp.dot(table, gext[r0 : r0 + 2 * taps, c], preferred_element_type=F32)
            owner = lax.broadcasted_iota(jnp.int32, (size, ct), 1) // gsize
            mixed = full[0:size]
            for k in range(1, gpt):
                mixed = jnp.where(owner == k, full[k * size : (k + 1) * size], mixed)
            gated = gext[taps + r0 : taps + r0 + size, c].astype(F32)
            mixed = mixed + skip[:, c] * gated
            hid[r0 : r0 + size, c] = (feature(0, r0, r0 + size, c) * mixed).astype(BF16)

    def send_part(part, r0, r1):
        for d in range(n_chan - 1, 0, -1):

            @pl.loop(0, oc // ot)
            def _(j):
                psend[d - 1, r0:r1, col(j, ot)] = jnp.dot(
                    hid[r0:r1, :], wo[d, :, col(j, ot)], preferred_element_type=F32
                ).astype(BF16)

            rs_copy(part, r0, r1, d).start()

    for d in range(n_chan):
        wo_copy(d).wait()
    starts = list(range(0, rows, taps))
    for r0 in starts[:0:-1]:
        long_filter(r0, min(taps, rows - r0))
    parts = [(taps, rows), (0, taps)]
    send_part(0, *parts[0])

    @pl.when(seq > 0)
    def _():
        halo_copy(1).wait_recv()

    long_filter(0, taps)
    send_part(1, *parts[1])

    for part, (r0, r1) in enumerate(parts):
        for d in range(n_chan - 1, 0, -1):
            rs_copy(part, r0, r1, d).wait_recv()

        @pl.loop(0, oc // ot)
        def _(j):
            c = col(j, ot)
            total = jnp.dot(hid[r0:r1, :], wo[0, :, c], preferred_element_type=F32)
            for d in range(1, n_chan):
                total = total + precv[d - 1, r0:r1, c].astype(F32)
            out[r0:r1, c] = total.astype(BF16)

    for d in range(1, n_chan):
        ag_copy(d).wait_send()
        for part, (r0, r1) in enumerate(parts):
            rs_copy(part, r0, r1, d).wait_send()

    @pl.when(seq < n_seq - 1)
    def _():
        halo_copy(0).wait_send()
        halo_copy(1).wait_send()


def solution(mesh):
    n_seq, n_chan = mesh.shape["seq"], mesh.shape["chan"]

    def body(tokens, in_weight, short_filter, long_filter, skip_gain, out_weight):
        rows, kc = tokens.shape
        cc = in_weight.shape[2]
        oc = out_weight.shape[1] // n_chan
        groups, taps = long_filter.shape
        streams = jnp.transpose(in_weight, (1, 0, 2))
        ext = taps + -(-rows // taps) * taps
        vmem = pl.BlockSpec(memory_space=pltpu.VMEM)
        hbm = pl.BlockSpec(memory_space=pl.ANY)
        dma = pltpu.SemaphoreType.DMA
        peers = n_chan - 1
        return pl.pallas_call(
            functools.partial(kernel, n_seq, n_chan),
            out_shape=jax.ShapeDtypeStruct((rows, oc), BF16),
            in_specs=[vmem, hbm, vmem, vmem, vmem, hbm],
            out_specs=vmem,
            scratch_shapes=[
                pltpu.VMEM((peers, rows, kc), BF16),
                pltpu.VMEM((n_chan, 3, kc, cc), BF16),
                pltpu.VMEM((n_chan, cc, oc), BF16),
                pltpu.VMEM((3, PAD + rows, cc), F32),
                pltpu.VMEM((rows, 128), F32),
                pltpu.VMEM((groups, 2 * taps), F32),
                pltpu.VMEM((groups, taps, 2 * taps), BF16),
                pltpu.VMEM((ext, cc), BF16),
                pltpu.VMEM((3, 16, cc), BF16),
                pltpu.VMEM((3, 16, cc), BF16),
                pltpu.VMEM((rows, cc), BF16),
                pltpu.VMEM((peers, rows, oc), BF16),
                pltpu.VMEM((peers, rows, oc), BF16),
                dma((n_chan,)),
                dma((n_chan,)),
                dma((peers,)),
                dma((peers,)),
                dma((2, peers)),
                dma((2, peers)),
                dma((2,)),
                dma((2,)),
            ],
            compiler_params=pltpu.CompilerParams(
                collective_id=0, has_side_effects=True, vmem_limit_bytes=62 * 2**20
            ),
            cost_estimate=pl.CostEstimate(
                flops=2 * rows * cc * (kc * n_chan * 3 + oc * n_chan),
                bytes_accessed=2 * (in_weight.size + out_weight.size),
                transcendentals=0,
            ),
        )(tokens, streams, short_filter, long_filter, skip_gain.reshape(1, cc), out_weight)

    in_specs = (
        P("seq", "chan"),
        P(None, None, "chan"),
        P(None, None, "chan"),
        P("chan", None),
        P("chan"),
        P("chan", None),
    )
    return jax.shard_map(body, mesh=mesh, in_specs=in_specs, out_specs=P("seq", "chan"), check_vma=False)
```

time: 281 us -> 84.1 us (0.30)
  local copies, waits for them, and re-layouts: 166 us -> 1.97 us
  Pallas kernels: 0 us -> 81.9 us
  waiting for transfers between devices: 52.5 us -> 0 us
  matrix products: 31.6 us -> 0 us
  between operations: 13.6 us -> 0.01 us
  other arithmetic: 8.77 us -> 0 us
  loops' own time: 3.43 us -> 0 us
    pallas_call x0 -> x1, Pallas kernels: none -> 81.9 us  [body(): pl.pallas_call(functools.partial(kernel, n_seq, n_chan), out_shape=jax.Sh...]
    dynamic_update_slice x5 -> x0, local copies, waits for them, and re-layouts: 72.9 us -> none  [body(): lax.map(one_block, jnp.arange(row_count // block_rows, dtype=jnp.int32))]
    gather x3 -> x0, local copies, waits for them, and re-layouts: 47.3 us -> none  [body(): jnp.take(long_filter, jnp.clip(lag_table, 0, filter_reach), axis=1)]
    reduce_scatter x1 -> x0, waiting for transfers between devices: 39.5 us -> none  [body(): lax.psum_scatter(partial_terms.astype(jnp.bfloat16), 'chan', scatter_dime...]
    unnamed x14 -> x1, local copies, waits for them, and re-layouts: 34.6 us -> 1.97 us
    dot_general x7 -> x0, matrix products: 31.6 us -> none  [the longest x1 13.9 us: body(): summed = jnp.dot(panel, flat_weight, preferred_element_type=jnp.float32)]
    all_gather x1 -> x0, waiting for transfers between devices: 12.3 us -> none  [body(): panel = lax.all_gather(tokens, 'chan', axis=1, tiled=True)]
    reshape x2 -> x0, local copies, waits for them, and re-layouts: 4.81 us -> none  [body(): lax.map(one_block, jnp.arange(row_count // block_rows, dtype=jnp.int32))]
  transfers between devices with their start and end apart: 3 -> 0, of which waited for: 2 -> 0; matrix products, arithmetic and copies ran while one was open for 29% -> 0% of each run, Pallas kernels for 0% -> 0%
where the time goes in v1:
time: 84.1 us; the launch traced here: 83.9 us
  Pallas kernels  81.9 us (97%)
  local copies, waits for them, and re-layouts  1.97 us (2%)
    pallas_call x1, Pallas kernels, body(): pl.pallas_call(functools.partial(kernel, n_seq, n_chan), out_shape=jax.Sh...  81.9 us
    unnamed x1, local copies, waits for them, and re-layouts  1.97 us

profile of v1, /device:TPU:0, one launch (start us, length us, event | category | flops | bytes accessed | tf_op | source)
XLA Modules:
  0.0 83.9 jit_solution(7349754936858663594)
XLA Ops:
  0.0 81.9 %shard_map.64 = bf16[320,1024]{1,0:T(8,128)(2,1)} custom-call(bf16[320,1024]{1,0:T(8,128)(2,1)} %tok.1, bf16[3,4096,1024]{2,1,0:T(8,128)(2,1)} %bitcast.2, f32[3,3,1024]{2,1,0:T(4,128)} %sf.1, bf16[64,128]{1,0:T(8,128)(2,1)} %lf.1, f32[1,1024]{1,0:T(1,128)} %bitcast.3, bf16[1024,4096]{1,0:T(8,128)(2,1)} %wo_hbm.1), custom_call_target="tpu_custom_call" | custom-call | flops 10737418240 | bytes 33554432 | tf_op jit(solution)/shard_map/pallas_call | solution.py:278
  82.0 2.0 %copy.8 = bf16[320,1024]{1,0:T(8,128)(2,1)} copy(bf16[320,1024]{1,0:T(8,128)(2,1)} %shard_map.64) | data formatting | bytes 1310720

commit v2 on v1

--- a/solution.py
+++ b/solution.py
@@ -14,7 +14,7 @@
 
 def kernel(
     n_seq, n_chan, tok, w_hbm, sf, lf, skip, wo_hbm, out,
-    panel, wv, wo, acc, ssq, rev, toep, gext, tail, halo_p, hid, psend, precv,
+    panel, wv, wo, acc, ssq, rev, toep, gext, tail, halo_p, hid, psend, precv, relay,
     w_sem, wo_sem, ag_send, ag_recv, rs_send, rs_recv, halo_send, halo_recv,
 ):
     rows, kc = tok.shape
@@ -52,12 +52,50 @@
             wo_hbm.at[:, pl.ds(pl.multiple_of(target[d] * oc, oc), oc)], wo.at[d], wo_sem.at[d]
         )
 
-    def ag_copy(d):
+    square = width == 2 and height == 2
+    top, bottom = pl.ds(0, rows // 2), pl.ds(rows // 2, rows // 2)
+    left, right = pl.ds(0, oc // 2), pl.ds(oc // 2, oc // 2)
+
+    def push(src, dst, send, recv, d):
         return pltpu.make_async_remote_copy(
-            src_ref=tok, dst_ref=panel.at[d - 1],
-            send_sem=ag_send.at[d - 1], recv_sem=ag_recv.at[d - 1],
+            src_ref=src, dst_ref=dst, send_sem=send, recv_sem=recv,
             device_id=(seq, target[d]), device_id_type=MESH,
         )
+
+    def ag_copy(k):
+        if square:
+            src, dst, d = (
+                (tok.at[top], panel.at[0, top], 1),
+                (tok.at[bottom], panel.at[1, bottom], 2),
+                (tok.at[bottom], panel.at[0, bottom], 1),
+                (tok.at[top], panel.at[1, top], 2),
+                (panel.at[0, top], panel.at[2, top], 2),
+                (panel.at[1, bottom], panel.at[2, bottom], 1),
+            )[k]
+        else:
+            src, dst, d = tok, panel.at[k], k + 1
+        return push(src, dst, ag_send.at[k], ag_recv.at[k], d)
+
+    def rs_copy(part, k):
+        r0, r1 = parts[part]
+        r = pl.ds(r0, r1 - r0)
+        if square:
+            src, dst, d = (
+                (psend.at[2, r, left], relay.at[0, r], 1),
+                (psend.at[2, r, right], relay.at[1, r], 2),
+                (psend.at[0, r, left], precv.at[0, r, left], 1),
+                (psend.at[1, r, right], precv.at[1, r, right], 2),
+                (psend.at[1, r, left], precv.at[1, r, left], 2),
+                (psend.at[0, r, right], precv.at[0, r, right], 1),
+            )[k]
+        else:
+            src, dst, d = psend.at[k, r], precv.at[k, r], k + 1
+        return push(src, dst, rs_send.at[part, k], rs_recv.at[part, k], d)
+
+    ag_count = rs_count = 6 if square else n_chan - 1
+    arriving = 2 if square else n_chan - 1
+    starts = list(range(0, rows, taps))
+    parts = [(r0, min(rows, r0 + taps)) for r0 in starts[::-1]]
 
     def halo_copy(which):
         src, dst = (
@@ -69,13 +107,6 @@
             device_id=(lax.rem(seq + 1, n_seq), chan), device_id_type=MESH,
         )
 
-    def rs_copy(part, r0, r1, d):
-        return pltpu.make_async_remote_copy(
-            src_ref=psend.at[d - 1, pl.ds(r0, r1 - r0)], dst_ref=precv.at[d - 1, pl.ds(r0, r1 - r0)],
-            send_sem=rs_send.at[part, d - 1], recv_sem=rs_recv.at[part, d - 1],
-            device_id=(seq, target[d]), device_id_type=MESH,
-        )
-
     w_copy(0).start()
     barrier = pltpu.get_barrier_semaphore()
     for d in range(1, n_chan):
@@ -92,8 +123,8 @@
     arrivals = n_chan - 1 + (seq > 0).astype(jnp.int32) + (seq < n_seq - 1).astype(jnp.int32)
     pl.semaphore_wait(barrier, arrivals)
 
-    for d in range(n_chan - 1, 0, -1):
-        ag_copy(d).start()
+    for k in range(4 if square else ag_count):
+        ag_copy(k).start()
     for d in range(1, n_chan):
         w_copy(d).start()
     for d in range(n_chan):
@@ -119,6 +150,12 @@
                 tok[...], wv[0, i, :, col(j, ct)], preferred_element_type=F32
             )
 
+    if square:
+        ag_copy(0).wait_recv()
+        ag_copy(4).start()
+        ag_copy(1).wait_recv()
+        ag_copy(5).start()
+
     lag = lax.broadcasted_iota(jnp.int32, (taps, 2 * taps), 0)
     place = lax.broadcasted_iota(jnp.int32, (taps, 2 * taps), 1)
     flip = jnp.where(lag + place == taps, 1.0, 0.0).astype(BF16)
@@ -134,7 +171,8 @@
     )
 
     for d in range(1, n_chan):
-        ag_copy(d).wait_recv()
+        for k in ((2,), (3,), (4, 5))[d - 1] if square else (d - 1,):
+            ag_copy(k).wait_recv()
         w_copy(d).wait()
         add_squares(panel.at[d - 1], False)
         if d < n_chan - 1:
@@ -212,48 +250,71 @@
             mixed = mixed + skip[:, c] * gated
             hid[r0 : r0 + size, c] = (feature(0, r0, r0 + size, c) * mixed).astype(BF16)
 
-    def send_part(part, r0, r1):
-        for d in range(n_chan - 1, 0, -1):
-
-            @pl.loop(0, oc // ot)
+    def send_part(part):
+        r0, r1 = parts[part]
+
+        def partial(d, first, count):
+            @pl.loop(first // ot, (first + count) // ot)
             def _(j):
                 psend[d - 1, r0:r1, col(j, ot)] = jnp.dot(
                     hid[r0:r1, :], wo[d, :, col(j, ot)], preferred_element_type=F32
                 ).astype(BF16)
 
-            rs_copy(part, r0, r1, d).start()
+        if square:
+            partial(3, 0, oc)
+            rs_copy(part, 0).start()
+            rs_copy(part, 1).start()
+            partial(1, 0, oc)
+            rs_copy(part, 2).start()
+            partial(2, 0, oc)
+            rs_copy(part, 3).start()
+        else:
+            for d in range(n_chan - 1, 0, -1):
+                partial(d, 0, oc)
+                rs_copy(part, d - 1).start()
+
+    def relay_part(part):
+        r0, r1 = parts[part]
+        for k, slot, c in ((0, 1, left), (1, 0, right)):
+            rs_copy(part, k).wait_recv()
+            psend[slot, r0:r1, c] = (
+                psend[slot, r0:r1, c].astype(F32) + relay[k, r0:r1].astype(F32)
+            ).astype(BF16)
+            rs_copy(part, 4 + k).start()
 
     for d in range(n_chan):
         wo_copy(d).wait()
-    starts = list(range(0, rows, taps))
-    for r0 in starts[:0:-1]:
-        long_filter(r0, min(taps, rows - r0))
-    parts = [(taps, rows), (0, taps)]
-    send_part(0, *parts[0])
-
-    @pl.when(seq > 0)
-    def _():
-        halo_copy(1).wait_recv()
-
-    long_filter(0, taps)
-    send_part(1, *parts[1])
-
     for part, (r0, r1) in enumerate(parts):
-        for d in range(n_chan - 1, 0, -1):
-            rs_copy(part, r0, r1, d).wait_recv()
+        if r0 == 0:
+
+            @pl.when(seq > 0)
+            def _():
+                halo_copy(1).wait_recv()
+
+        long_filter(r0, r1 - r0)
+        send_part(part)
+        if square and part > 0:
+            relay_part(part - 1)
+    if square:
+        relay_part(len(parts) - 1)
+
+    for part, (r0, r1) in enumerate(parts):
+        for k in range(2, 6) if square else range(rs_count):
+            rs_copy(part, k).wait_recv()
 
         @pl.loop(0, oc // ot)
         def _(j):
             c = col(j, ot)
             total = jnp.dot(hid[r0:r1, :], wo[0, :, c], preferred_element_type=F32)
-            for d in range(1, n_chan):
-                total = total + precv[d - 1, r0:r1, c].astype(F32)
+            for k in range(arriving):
+                total = total + precv[k, r0:r1, c].astype(F32)
             out[r0:r1, c] = total.astype(BF16)
 
-    for d in range(1, n_chan):
-        ag_copy(d).wait_send()
-        for part, (r0, r1) in enumerate(parts):
-            rs_copy(part, r0, r1, d).wait_send()
+    for k in range(ag_count):
+        ag_copy(k).wait_send()
+    for part in range(len(parts)):
+        for k in range(rs_count):
+            rs_copy(part, k).wait_send()
 
     @pl.when(seq < n_seq - 1)
     def _():
@@ -294,12 +355,13 @@
                 pltpu.VMEM((rows, cc), BF16),
                 pltpu.VMEM((peers, rows, oc), BF16),
                 pltpu.VMEM((peers, rows, oc), BF16),
+                pltpu.VMEM((2, rows, oc // 2), BF16),
                 dma((n_chan,)),
                 dma((n_chan,)),
-                dma((peers,)),
-                dma((peers,)),
-                dma((2, peers)),
-                dma((2, peers)),
+                dma((max(6, peers),)),
+                dma((max(6, peers),)),
+                dma((-(-rows // taps), max(6, peers))),
+                dma((-(-rows // taps), max(6, peers))),
                 dma((2,)),
                 dma((2,)),
             ],

time: 84.1 us -> 63.5 us (0.76)
  Pallas kernels: 81.9 us -> 61.3 us
    pallas_call x1, Pallas kernels: 81.9 us -> 61.3 us  [body(): pl.pallas_call(functools.partial(kernel, n_seq, n_chan), out_shape=jax.Sh...]
where the time goes in v2:
time: 63.5 us; the launch traced here: 63.3 us
  Pallas kernels  61.3 us (97%)
  local copies, waits for them, and re-layouts  1.97 us (3%)
    pallas_call x1, Pallas kernels, body(): pl.pallas_call(functools.partial(kernel, n_seq, n_chan), out_shape=jax.Sh...  61.3 us
    unnamed x1, local copies, waits for them, and re-layouts  1.97 us

profile of v2, /device:TPU:0, one launch (start us, length us, event | category | flops | bytes accessed | tf_op | source)
XLA Modules:
  0.0 63.3 jit_solution(9481828576219512667)
XLA Ops:
  0.0 61.3 %shard_map.64 = bf16[320,1024]{1,0:T(8,128)(2,1)} custom-call(bf16[320,1024]{1,0:T(8,128)(2,1)} %tok.1, bf16[3,4096,1024]{2,1,0:T(8,128)(2,1)} %bitcast.2, f32[3,3,1024]{2,1,0:T(4,128)} %sf.1, bf16[64,128]{1,0:T(8,128)(2,1)} %lf.1, f32[1,1024]{1,0:T(1,128)} %bitcast.3, bf16[1024,4096]{1,0:T(8,128)(2,1)} %wo_hbm.1), custom_call_target="tpu_custom_call" | custom-call | flops 10737418240 | bytes 33554432 | tf_op jit(solution)/shard_map/pallas_call | solution.py:339
  61.3 2.0 %copy.8 = bf16[320,1024]{1,0:T(8,128)(2,1)} copy(bf16[320,1024]{1,0:T(8,128)(2,1)} %shard_map.64) | data formatting | bytes 1310720
